TPU v7x, 128 devices: a whole 4x4x4 slice. The times are simulated.
128 devices in a mesh: replica: 8 (over x_lo, z), fsdp: 16 (over x_hi, y, core).
Axes of the slice: x: 4 (x_hi: 2, x_lo: 2; x = x_hi * 2 + x_lo), y: 4, z: 4, core: 2. Of those that a mesh axis runs over, the one named last changes fastest.
Arguments:
- queries: bfloat16 [32768, 2048], P(('replica', 'fsdp')), may hold values from -6 to 6
- keys: bfloat16 [32768, 2048], P(('replica', 'fsdp')), may hold values from -6 to 6
- values: bfloat16 [32768, 2048], P(('replica', 'fsdp')), may hold values from -6 to 6
- log_decay: float32 [16, 32768], P(None, ('replica', 'fsdp')), may hold values from -1 to 0, as said below
- write_strength: float32 [16, 32768], P(None, ('replica', 'fsdp')), may hold values from 0.1 to 1
- out_grad: bfloat16 [32768, 4096], P(('replica', 'fsdp')), may hold values from -6 to 6
- replica_weights: float32 [8, 2048, 4096], P('replica', 'fsdp'), may hold values from -8 to 8
- adam_first: float32 [8, 2048, 4096], P('replica', 'fsdp'), may hold values from -1.5 to 1.5
- adam_second: float32 [8, 2048, 4096], P('replica', 'fsdp'), may hold values from 0.05 to 0.5
- anchor: float32 [2048, 4096], P('fsdp'), may hold values from -6 to 6
- outer_momentum: float32 [2048, 4096], P('fsdp'), may hold values from -0.3125 to 0.3125
- exponents: int32 [8, 16], P('replica', 'fsdp'), may hold values from -13 to -11
Outputs:
- layer_out: bfloat16 [32768, 4096], P(('replica', 'fsdp'))
- new_anchor: float32 [2048, 4096], P('fsdp')
- new_momentum: float32 [2048, 4096], P('fsdp')
Inputs may be any that keep to these rules, and one draw needn't show every extreme that they name: `log_decay`: negative.
All inputs are finite; a program needn't handle non-finite values.
Results may differ from a plain program's by a relative error of at most 0.0057.
Values may be sent and summed in bfloat16 or wider, within the bound.
A program may use at most 128 MiB of HBM per device.

v0:
```python
import jax
import jax.numpy as jnp
from jax import lax
from jax.sharding import PartitionSpec as P

OWNED_ATTN_UNITS = 16
HEAD = 128
GROUP = 128
BLOCK = 128


HIGH = lax.Precision.HIGHEST


def unit_lower_apply(couple, sides):
    negated = -couple
    result = sides + jnp.einsum("hnij,hnjc->hnic", negated, sides, precision=HIGH)
    reach = 2
    power = negated
    while reach < couple.shape[-1]:
        power = jnp.einsum("hnij,hnjk->hnik", power, power, precision=HIGH)
        result = result + jnp.einsum("hnij,hnjc->hnic", power, result, precision=HIGH)
        reach = reach * 2
    return result


def delta_core(queries, keys, values, log_decay, write_strength):
    length = queries.shape[0]
    blocks = length // GROUP

    def arrange(item):
        return (
            item.astype(jnp.float32)
            .reshape(blocks, GROUP, OWNED_ATTN_UNITS, HEAD)
            .transpose(2, 0, 1, 3)
        )

    qf, kf, vf = (arrange(queries), arrange(keys), arrange(values))
    kn = kf / jnp.sqrt(jnp.sum(kf * kf, axis=-1, keepdims=True) + 1e-06)
    qs = qf * HEAD ** (-0.5)
    strength = write_strength.reshape(OWNED_ATTN_UNITS, blocks, GROUP)
    decay_sum = jnp.cumsum(log_decay.reshape(OWNED_ATTN_UNITS, blocks, GROUP), axis=-1)
    gaps = decay_sum[..., :, None] - decay_sum[..., None, :]
    places = jnp.arange(GROUP)
    lower = places[:, None] > places[None, :]
    lower_eq = places[:, None] >= places[None, :]
    fades = jnp.where(lower_eq, jnp.exp(jnp.where(lower_eq, gaps, 0.0)), 0.0)
    key_key = jnp.einsum("hnik,hnjk->hnij", kn, kn, precision=HIGH)
    couple = jnp.where(lower, fades * key_key, 0.0) * strength[..., :, None]
    growth = jnp.exp(decay_sum)
    sides = jnp.concatenate(
        ((strength * growth)[..., None] * kn, strength[..., None] * vf), axis=-1
    )
    solved = unit_lower_apply(couple, sides)
    wide, base = (solved[..., :HEAD], solved[..., HEAD:])
    mixing = fades * jnp.einsum("hnik,hnjk->hnij", qs, kn, precision=HIGH)
    closing = jnp.exp(decay_sum[..., -1:] - decay_sum)
    state = jnp.zeros((OWNED_ATTN_UNITS, HEAD, HEAD), jnp.float32)
    results = []
    for index in range(blocks):
        fresh = base[:, index] - jnp.einsum("hck,hvk->hcv", wide[:, index], state, precision=HIGH)
        carried = jnp.einsum("hck,hvk->hcv", qs[:, index], state, precision=HIGH)
        output = growth[:, index][..., None] * carried + jnp.einsum(
            "hti,hiv->htv", mixing[:, index], fresh, precision=HIGH
        )
        results.append(output)
        weighted = fresh * closing[:, index][..., None]
        state = jnp.exp(decay_sum[:, index, -1])[:, None, None] * state + jnp.einsum(
            "hiv,hik->hvk", weighted, kn[:, index], precision=HIGH
        )
    stacked = jnp.stack(results, axis=1)
    return (
        stacked.transpose(1, 2, 0, 3).reshape(length, OWNED_ATTN_UNITS * HEAD).astype(jnp.bfloat16)
    )


def on_device(
    queries,
    keys,
    values,
    log_decay,
    write_strength,
    out_grad,
    replica_weights,
    adam_first,
    adam_second,
    anchor,
    outer_momentum,
    exponents,
):
    core = delta_core(queries, keys, values, log_decay, write_strength)
    width = core.shape[1]
    scale = width ** (-0.5)
    working = replica_weights[0].astype(jnp.bfloat16)
    columns = core
    projected = jnp.dot(
        columns,
        lax.all_gather(working, "fsdp", axis=0, tiled=True),
        preferred_element_type=jnp.float32,
    )
    layer_out = (projected * scale).astype(jnp.bfloat16)
    columns = core
    term = lax.dot_general(
        columns, out_grad, (((0,), (0,)), ((), ())), preferred_element_type=jnp.float32
    )
    grad = lax.psum_scatter(
        (term * scale).astype(jnp.bfloat16), "fsdp", scatter_dimension=0, tiled=True
    ).astype(jnp.float32)
    weights = replica_weights[0]
    first = 0.9 * adam_first[0] + 0.1 * grad
    second = 0.95 * adam_second[0] + 0.05 * grad * grad
    updated = weights - 0.03 * (first / (jnp.sqrt(second) + 1e-08) + 0.1 * weights)
    delta = anchor - updated
    rows_here, columns_here = delta.shape
    blocks_here = rows_here // BLOCK
    power = exponents[0].astype(jnp.float32)
    down_scale = jnp.exp2(-power)
    up_scale = jnp.exp2(power)
    shaped = delta.reshape(blocks_here, BLOCK, columns_here)
    encoded = jnp.clip(shaped * down_scale[:, None, None], -448.0, 448.0).astype(jnp.bfloat16)
    every_code, every_scale = (
        lax.all_gather(encoded[None], "replica", axis=0, tiled=True),
        lax.all_gather(up_scale.astype(jnp.bfloat16)[None], "replica", axis=0, tiled=True),
    )
    decoded = every_code.astype(jnp.float32) * every_scale.astype(jnp.float32)[:, :, None, None]
    total = jnp.sum(decoded, axis=0)
    outer_delta = total.reshape(rows_here, columns_here) / lax.axis_size("replica")
    new_momentum = 0.9 * outer_momentum + outer_delta
    new_anchor = anchor - 0.7 * (outer_delta + 0.9 * new_momentum)
    return (layer_out, new_anchor, new_momentum)


def solution(mesh):
    return jax.shard_map(
        on_device,
        mesh=mesh,
        in_specs=(
            P(("replica", "fsdp"), None),
            P(("replica", "fsdp"), None),
            P(("replica", "fsdp"), None),
            P(None, ("replica", "fsdp")),
            P(None, ("replica", "fsdp")),
            P(("replica", "fsdp"), None),
            P("replica", "fsdp", None),
            P("replica", "fsdp", None),
            P("replica", "fsdp", None),
            P("fsdp", None),
            P("fsdp", None),
            P("replica", "fsdp"),
        ),
        out_specs=(P(("replica", "fsdp"), None), P("fsdp", None), P("fsdp", None)),
        check_vma=False,
    )
```

profile of v0, /device:TPU:1, one launch (start us, length us, event | category | flops | bytes accessed | tf_op | source)
XLA Modules:
  0.0 462.4 jit_solution(3317281038760154719)
XLA Ops:
  7.2 0.9 copy_bitcast_fusion.1
  8.1 0.7 reshape.79
  8.8 0.6 reduce_window_sum.11
  9.4 0.7 fusion.42
  10.5 1.4 convert_bitcast_fusion.1
  12.0 0.4 copy.38
  12.4 1.0 fusion.17
  13.9 0.4 copy.39
  14.2 2.6 broadcast_multiply_fusion
  16.8 4.8 %multiply_negate_fusion = f32[16,2,128,128]{3,2,1,0:T(8,128)S(1)} fusion(f32[16,2,128,128]{3,2,1,0:T(8,128)S(1)} %get-tuple-element.6, f32[16,2,128]{2,1,0:T(2,128)S(1)} %reshape.79, f32[16,2,128]{2,1,0:T(2,128)S(1)} %copy.24, pred[128,128]{1,0:T(8,128)(4,1)S(1)} %get-tuple-element.11, pred[128,128]{1,0:T(8,128)(4,1)S(1)} %get-tuple-element.12), kind=kOutput, calls=%fused_computation.40 | convolution fusion | flops 808976384 | bytes 4259840 | tf_op jit(solution)/shard_map/hnik,hnjk->hnij/dot_general | solution.py:48
  21.6 2.2 fusion.43
  23.8 2.2 fusion.45
  26.0 4.4 fusion.2
  30.4 4.5 fusion.44
  34.9 2.2 fusion.46
  37.1 4.7 %convolution_add_fusion.2 = f32[16,2,128,256]{3,2,1,0:T(8,128)S(1)} fusion(f32[16,2,128,128]{3,2,1,0:T(8,128)S(1)} %fusion.45, f32[16,2,128,256]{3,2,1,0:T(8,128)S(1)} %fusion.2, f32[16,2,128,256]{3,2,1,0:T(8,128)S(1)} %fusion.44), kind=kOutput, calls=%fused_computation.13 | convolution fusion | flops 1612709888 | bytes 14680064 | tf_op jit(solution)/shard_map/hnij,hnjc->hnic/dot_general | solution.py:22
  41.8 2.6 fusion.48
  44.4 4.3 fusion.47
  48.7 2.2 fusion.49
  50.9 4.7 %convolution_add_fusion.1 = f32[16,2,128,256]{3,2,1,0:T(8,128)S(1)} fusion(f32[16,2,128,128]{3,2,1,0:T(8,128)S(1)} %fusion.48, f32[16,2,128,256]{3,2,1,0:T(8,128)S(1)} %convolution_add_fusion.2, f32[16,2,128,256]{3,2,1,0:T(8,128)S(1)} %fusion.47), kind=kOutput, calls=%fused_computation.11 | convolution fusion | flops 1612709888 | bytes 14680064 | tf_op jit(solution)/shard_map/hnij,hnjc->hnic/dot_general | solution.py:22
  55.6 2.4 fusion.51
  58.0 4.3 fusion.50
  62.3 4.7 %convolution_add_fusion = f32[16,2,128,256]{3,2,1,0:T(8,128)S(1)} fusion(f32[16,2,128,128]{3,2,1,0:T(8,128)S(1)} %fusion.51, f32[16,2,128,256]{3,2,1,0:T(8,128)S(1)} %convolution_add_fusion.1, f32[16,2,128,256]{3,2,1,0:T(8,128)S(1)} %fusion.50), kind=kOutput, calls=%fused_computation.9 | convolution fusion | flops 1612709888 | bytes 14680064 | tf_op jit(solution)/shard_map/hnij,hnjc->hnic/dot_general | solution.py:22
  67.1 1.0 convolution_subtract_fusion.1
  68.3 0.2 multiply_bitcast_fusion
  68.5 0.4 copy.37
  69.1 5.3 %fusion.20 = f32[16,2,128,128]{3,2,1,0:T(8,128)S(1)} fusion(f32[16,2,128,128]{3,2,1,0:T(8,128)S(1)} %get-tuple-element.6, f32[16,2,128,128]{3,0,2,1:T(8,128)S(1)} %bitcast_bitcast_fusion, f32[16,2,128]{2,1,0:T(2,128)S(1)} %copy.24, pred[128,128]{1,0:T(8,128)(4,1)S(1)} %get-tuple-element.12), kind=kOutput, calls=%fused_computation.42 | convolution fusion | flops 807403520 | bytes 6324224 | tf_op jit(solution)/shard_map/hnik,hnjk->hnij/dot_general | solution.py:56
  74.4 0.6 copy.60
  75.1 2.2 convolution_add_fusion.4
  77.4 2.3 convolution_subtract_fusion
  79.7 1.0 convolution_multiply_fusion.2
  80.7 2.3 convolution_multiply_fusion.1
  83.0 1.2 fusion.26
  84.3 1.3 fusion.25
  85.5 0.4 maximum_bitcast_fusion
  85.9 0.7 copy.32
  86.6 8.2 %multiply_convert_fusion = bf16[2048,4096]{1,0:T(8,128)(2,1)} fusion(bf16[256,4096]{1,0:T(8,128)(2,1)S(1)} %copy-done, bf16[32,8,16,128]{3,2,1,0:T(8,128)(2,1)S(1)} %bitcast.145), kind=kOutput, calls=%fused_computation | convolution fusion | flops 4311744512 | bytes 19922944 | tf_op jit(solution)/shard_map/dot_general | solution.py:103
  94.9 2.7 bitcast_convert_fusion
  98.3 146.1 %reduce-scatter.2.cloned.1.call-done = bf16[128,4096]{1,0:T(8,128)(2,1)} async-done(((bf16[2048,4096]{1,0:T(8,128)(2,1)}), bf16[128,4096]{1,0:T(8,128)(2,1)}) %reduce-scatter.2.cloned.1.call-update) | async-done | bytes 1048592 | tf_op jit(solution)/shard_map/reduce_scatter | solution.py:106
  244.4 6.5 %clamp_convert_fusion = bf16[128,4096]{1,0:T(8,128)(2,1)} fusion(f32[128,4096]{1,0:T(8,128)} %param.21, f32[1,128,4096]{2,1,0:T(8,128)} %param.20, bf16[128,4096]{1,0:T(8,128)(2,1)} %reduce-scatter.2.cloned.1.call-done, f32[1,128,4096]{2,1,0:T(8,128)} %param.19, f32[1,128,4096]{2,1,0:T(8,128)} %param.18, f32[]{:T(128)} %bitcast.22), kind=kLoop, calls=%fused_computation.39 | loop fusion | flops 9437184 | bytes 10485764 | tf_op jit(solution)/shard_map/convert_element_type | solution.py:120
  251.0 0.6 dynamic-slice
  251.6 0.7 dynamic-update-slice
  252.3 16.1 %all-reduce = bf16[8]{0:T(256)(128)(2,1)S(1)} all-reduce(bf16[8]{0:T(256)(128)(2,1)S(1)} %dynamic-update-slice), channel_id=1, replica_groups=mesh['replica'=8,'fsdp'=16] {'replica'}, use_global_device_ids=true, to_apply=%add | all-reduce | flops 8 | bytes 32
  268.4 87.1 %all-gather.4.cloned.1.call-done = bf16[2048,4096]{1,0:T(8,128)(2,1)} async-done(((bf16[128,4096]{1,0:T(8,128)(2,1)}), bf16[2048,4096]{1,0:T(8,128)(2,1)}) %all-gather.4.cloned.1.call-update) | async-done | bytes 16777232 | tf_op jit(solution)/shard_map/all_gather | solution.py:98
  355.5 11.5 %fusion.1 = bf16[256,4096]{1,0:T(8,128)(2,1)} fusion(bf16[2048,4096]{1,0:T(8,128)(2,1)} %all-gather.4.cloned.1.call-done, bf16[32,8,16,128]{3,2,1,0:T(8,128)(2,1)S(1)} %bitcast.146), kind=kOutput, calls=%fused_computation.4 | convolution fusion | flops 4297064448 | bytes 19922944 | tf_op jit(solution)/shard_map/dot_general | solution.py:96
  367.1 80.1 %all-gather.6.cloned.1.call-done = bf16[1024,4096]{1,0:T(8,128)(2,1)} async-done(((bf16[128,4096]{1,0:T(8,128)(2,1)}), bf16[1024,4096]{1,0:T(8,128)(2,1)}) %all-gather.6.cloned.1.call-update) | async-done | bytes 8388624 | tf_op jit(solution)/shard_map/all_gather | solution.py:122
  447.2 5.6 %fusion = f32[128,4096]{1,0:T(8,128)S(1)} fusion(bf16[8,1,128,4096]{3,2,0,1:T(8,128)(2,1)} %bitcast.144, f32[8]{0:T(128)S(1)} %mul.228), kind=kLoop, calls=%fused_computation.2 | loop fusion | flops 12058624 | bytes 10485792 | tf_op jit(solution)/shard_map/reduce_sum | solution.py:126
  452.9 2.6 multiply_subtract_fusion
  (31 shorter events, 1.5 us)
Async XLA Ops:
  7.2 79.4 %copy-start = (bf16[256,4096]{1,0:T(8,128)(2,1)S(1)}, bf16[256,4096]{1,0:T(8,128)(2,1)}, u32[]{:S(2)}) copy-start(bf16[256,4096]{1,0:T(8,128)(2,1)} %param.17) | copy-start | bytes 6291460
  7.2 237.3 %reduce-scatter.2.cloned.1.call-start = ((), (), s32[]{:S(2)}) async-start(), calls=%async_computation.2 | async-start | bytes 17825792 | tf_op jit(solution)/shard_map/reduce_scatter | solution.py:106
  12.4 1.2 copy-start.3
  67.1 1.2 copy-start.4
  94.8 260.7 %all-gather.4.cloned.1.call-start = ((), (), s32[]{:S(2)}) async-start(), calls=%async_computation.1 | async-start | bytes 17825792 | tf_op jit(solution)/shard_map/all_gather | solution.py:98
  97.6 349.6 %all-gather.6.cloned.1.call-start = ((), (), s32[]{:S(2)}) async-start(), calls=%async_computation.3 | async-start | bytes 9437184 | tf_op jit(solution)/shard_map/all_gather | solution.py:122
  244.4 6.6 %copy-start.5 = (u32[128]{0:T(128)S(1)}, u32[128]{0:T(128)}, u32[]{:S(2)}) copy-start(u32[128]{0:T(128)} %constant.44) | copy-start | bytes 1540
  447.2 5.6 %copy-start.1 = (f32[128,4096]{1,0:T(8,128)S(1)}, f32[128,4096]{1,0:T(8,128)}, u32[]{:S(2)}) copy-start(f32[128,4096]{1,0:T(8,128)} %param.21) | copy-start | bytes 6291460
  447.2 5.6 %copy-start.2 = (f32[128,4096]{1,0:T(8,128)S(1)}, f32[128,4096]{1,0:T(8,128)}, u32[]{:S(2)}) copy-start(f32[128,4096]{1,0:T(8,128)} %param.22) | copy-start | bytes 6291460
Sparse Core Ops, SparseCore 0:
  94.9 149.4 reduce-scatter.1
  247.5 107.9 all-gather.3
  357.7 89.4 all-gather.5
where the time goes:
time: 466 us; the launch traced here: 462 us
  waiting for transfers between devices  313 us (67%)
  matrix products  86.5 us (19%)
  other arithmetic  24.8 us (5%)
  blocking collectives  16.1 us (3%)
  between operations  15.3 us (3%)
  local copies, waits for them, and re-layouts  6.13 us (1%)
    reduce_scatter x1, waiting for transfers between devices, on_device(): lax.psum_scatter((term * scale).astype(jnp.bfloat16), 'fsdp', scatter_dim...  146 us
    all_gather x1, waiting for transfers between devices, on_device(): lax.all_gather(working, 'fsdp', axis=0, tiled=True)  87.1 us
    all_gather x1, waiting for transfers between devices, on_device(): lax.all_gather(encoded[None], 'replica', axis=0, tiled=True)  80.1 us
    dot_general x6, matrix products, unit_lower_apply(): jnp.einsum('hnij,hnjc->hnic', power, result, precision=HIGH)  27.3 us
    unnamed x1, blocking collectives  16.1 us
    dot_general x6, matrix products, unit_lower_apply(): power = jnp.einsum('hnij,hnjk->hnik', power, power, precision=HIGH)  13.7 us
    dot_general x1, matrix products, on_device(): jnp.dot(columns, lax.all_gather(working, 'fsdp', axis=0, tiled=True), pre...  11.5 us
  transfers between devices with their start and end apart: 3, of which 3 were waited for; matrix products, arithmetic and copies ran while one was open for 5% of the time, Pallas kernels for 0%

commit v1 on v0

v1 whole, which is shorter than its diff:
```python
import jax
import jax.numpy as jnp
from jax import lax
from jax.experimental import pallas as pl
from jax.experimental.pallas import tpu as pltpu
from jax.sharding import PartitionSpec as P

HEAD = 128
HEADS = 16
SEQ = 256
WIDTH = HEADS * HEAD
D = 4096
BLOCK = 128
REPLICAS = 8
SHARE = BLOCK // REPLICAS
GROUP = 4
GROUPS = HEADS // GROUP
CHUNK = 512
CHUNKS = D // CHUNK
HALF = CHUNK // 2
SIDE = D // 2
SCALE = WIDTH ** (-0.5)
SENDS = 2
F32 = jnp.float32
BF16 = jnp.bfloat16
NT = (((1,), (1,)), ((), ()))
MESH = pl.DeviceIdType.MESH


def split(item):
    high = item.astype(BF16)
    return high, (item - high.astype(F32)).astype(BF16)


def as_left(item):
    return jnp.concatenate(split(item), axis=1)


def as_right(item):
    row = jnp.concatenate(split(item), axis=1)
    return jnp.concatenate((row, row), axis=0)


def product(left, right):
    both = jnp.dot(left, right, preferred_element_type=F32)
    return both[:, :HEAD] + both[:, HEAD:]


def fill_tables(keys, log_decay, strength, rows, cols):
    i = lax.broadcasted_iota(jnp.int32, (SEQ, SEQ), 0)
    j = lax.broadcasted_iota(jnp.int32, (SEQ, SEQ), 1)
    upto = jnp.where(i <= j, 1.0, 0.0).astype(F32)
    sums = jnp.dot(
        log_decay[...], upto, preferred_element_type=F32, precision=lax.Precision.HIGHEST
    )
    ones = jnp.ones((8, HEAD), BF16)
    rows[...] = jnp.zeros_like(rows)
    for g in range(GROUPS):
        rows[g, 0:GROUP, :] = sums[g * GROUP : (g + 1) * GROUP]
        rows[g, GROUP : 2 * GROUP, :] = strength[g * GROUP : (g + 1) * GROUP, :]
        for n in range(GROUP):
            h = g * GROUP + n
            key = keys[:, h * HEAD : (h + 1) * HEAD].astype(F32)
            high, low = split(key * key)
            total = lax.dot_general(ones, high, NT, preferred_element_type=F32)
            total = total + lax.dot_general(ones, low, NT, preferred_element_type=F32)
            rows[g, 2 * GROUP + n : 2 * GROUP + n + 1, :] = lax.rsqrt(total[0:1] + 1e-6)
        cols[g] = rows[g].T


def delta_group(g, queries, keys, values, rows, cols):
    i = lax.broadcasted_iota(jnp.int32, (HEAD, HEAD), 0)
    j = lax.broadcasted_iota(jnp.int32, (HEAD, HEAD), 1)
    col = cols[g]
    low, strict = i >= j, i > j
    couple_1, couple_2, cross, mix_1, mix_2, mix_cross, sides = [], [], [], [], [], [], []
    for n in range(GROUP):
        at = pl.ds(pl.multiple_of((g * GROUP + n) * HEAD, HEAD), HEAD)
        query, key = queries[:, at], keys[:, at]
        decay_row = rows[g, n : n + 1, :]
        norm_row = rows[g, 2 * GROUP + n : 2 * GROUP + n + 1, :]
        decay_col = col[:, n : n + 1]
        strength = col[:, GROUP + n : GROUP + n + 1]
        scaled = strength * col[:, 2 * GROUP + n : 2 * GROUP + n + 1]
        dots = lax.dot_general(
            jnp.concatenate((key, query), axis=0), key, NT, preferred_element_type=F32
        )
        left_norm, right_norm = norm_row[:, :HEAD], norm_row[:, HEAD:]
        gap_1 = decay_col[:HEAD] - decay_row[:, :HEAD]
        gap_2 = decay_col[HEAD:] - decay_row[:, HEAD:]
        gap_cross = decay_col[HEAD:] - decay_row[:, :HEAD]
        fade_1 = jnp.exp(jnp.where(low, gap_1, -1e30)) * left_norm
        fade_2 = jnp.exp(jnp.where(low, gap_2, -1e30)) * right_norm
        fade_cross = jnp.exp(jnp.minimum(gap_cross, 0.0)) * left_norm
        couple_1.append(jnp.where(strict, dots[:HEAD, :HEAD] * fade_1 * scaled[:HEAD], 0.0))
        couple_2.append(jnp.where(strict, dots[HEAD:SEQ, HEAD:] * fade_2 * scaled[HEAD:], 0.0))
        cross.append(dots[HEAD:SEQ, :HEAD] * fade_cross * scaled[HEAD:])
        size = HEAD ** (-0.5)
        mix_1.append(dots[SEQ : SEQ + HEAD, :HEAD] * fade_1 * size)
        mix_2.append(dots[SEQ + HEAD :, HEAD:] * fade_2 * size)
        mix_cross.append(dots[SEQ + HEAD :, :HEAD] * fade_cross * size)
        sides.append(strength * values[:, at].astype(F32))
    couples = couple_1 + couple_2
    eye = jnp.where(i == j, 1.0, 0.0).astype(F32)
    inverse = [eye - jnp.where(i // 2 == j // 2, couple, 0.0) for couple in couples]
    size = 2
    while size < HEAD:
        below = (i // (2 * size) == j // (2 * size)) & (i % (2 * size) >= size) & (j % (2 * size) < size)
        lefts = [as_left(jnp.where(below, couple, 0.0)) for couple in couples]
        steps = [product(left, as_right(item)) for left, item in zip(lefts, inverse)]
        inverse = [item - product(as_left(item), as_right(step)) for item, step in zip(inverse, steps)]
        size *= 2
    results = []
    fresh_1 = [product(as_left(inverse[n]), as_right(sides[n][:HEAD])) for n in range(GROUP)]
    uses = [
        product(
            as_left(jnp.concatenate((cross[n], mix_1[n], mix_cross[n]), axis=0)), as_right(fresh_1[n])
        )
        for n in range(GROUP)
    ]
    fresh_2 = [
        product(as_left(inverse[GROUP + n]), as_right(sides[n][HEAD:] - uses[n][:HEAD]))
        for n in range(GROUP)
    ]
    for n in range(GROUP):
        second = uses[n][2 * HEAD :] + product(as_left(mix_2[n]), as_right(fresh_2[n]))
        results.append(jnp.concatenate((uses[n][HEAD : 2 * HEAD], second), axis=0))
    return results


def kernel(
    queries_hbm, keys_hbm, values_hbm, decay_hbm, strength_hbm, out_grad_hbm, weights_hbm,
    first_hbm, second_hbm, anchor_hbm, momentum_hbm, exponents,
    layer_out_hbm, new_anchor_hbm, new_momentum_hbm,
    queries, keys, values, decay, strength, weights, first, second, anchor, momentum,
    rows, cols, core, core_t, core_quad, grad_quad, every_weight, partial,
    relay_up, relay_down, sum_up, sum_down, decoded, shares, outer,
    load_sem, store_sem, grad_send, grad_recv, core_send, core_recv, row_send, row_recv,
    pair_send, pair_recv, relay_send, relay_recv, sum_send, sum_recv,
    share_send, share_recv, outer_send, outer_recv,
):
    replica, me = lax.axis_index("replica"), lax.axis_index("fsdp")
    x, y, c = me // 8, (me // 2) % 4, me % 2

    def index(x_at, y_at, c_at):
        return x_at * 8 + lax.rem(y_at + 4, 4) * 2 + c_at

    def device(f):
        return {"replica": replica, "fsdp": f}

    sibling, across, corner = index(x, y, 1 - c), index(1 - x, y, c), index(1 - x, y, 1 - c)
    up, down = index(x, y + 1, c), index(x, y - 1, c)
    others = [lax.rem(replica + k, REPLICAS) for k in range(1, REPLICAS)]
    member = x * 2 + c
    member_sibling, member_across, member_corner = x * 2 + 1 - c, (1 - x) * 2 + c, (1 - x) * 2 + 1 - c

    started = []

    def copy(src, dst, send_sem, recv_sem, to):
        return pltpu.make_async_remote_copy(
            src_ref=src, dst_ref=dst, send_sem=send_sem, recv_sem=recv_sem,
            device_id=to, device_id_type=MESH,
        )

    def send(src, dst, send_sem, recv_sem, to):
        item = copy(src, dst, send_sem, recv_sem, to)
        item.start()
        started.append(item)

    def arrived(region, recv_sem):
        copy(region, region, recv_sem, recv_sem, device(sibling)).wait_recv()

    grad_own = grad_quad.at[pl.ds(pl.multiple_of(member * SEQ, SEQ), SEQ)]
    loads = [
        (weights_hbm.at[0], weights), (keys_hbm, keys), (decay_hbm, decay), (strength_hbm, strength),
        (queries_hbm, queries), (values_hbm, values), (out_grad_hbm, grad_own), (first_hbm.at[0], first),
        (second_hbm.at[0], second), (anchor_hbm, anchor), (momentum_hbm, momentum),
    ]
    loads = [pltpu.make_async_copy(src, dst, load_sem.at[n]) for n, (src, dst) in enumerate(loads)]
    for load in loads:
        load.start()

    barrier = pltpu.get_barrier_semaphore()
    peers = [device(f) for f in (sibling, across, corner, up, down)]
    peers += [{"replica": r, "fsdp": me} for r in others]
    for peer in peers:
        pl.semaphore_signal(barrier, inc=1, device_id=peer, device_id_type=MESH)
    pl.semaphore_wait(barrier, len(peers))

    def grad_part(who, j):
        return grad_quad.at[
            pl.ds(pl.multiple_of(who * SEQ, SEQ), SEQ), pl.ds(j * CHUNK, CHUNK)
        ]

    def send_grad(j):
        src = out_grad_hbm.at[:, pl.ds(j * CHUNK, CHUNK)]
        send(src, grad_part(member, j), grad_send.at[0, j], grad_recv.at[0, j], device(across))
        send(src, grad_part(member, j), grad_send.at[1, j], grad_recv.at[1, j], device(sibling))

    def pass_grad(j):
        arrived(grad_part(member_across, j), grad_recv.at[0, j])
        send(
            grad_part(member_across, j), grad_part(member_across, j),
            grad_send.at[2, j], grad_recv.at[2, j], device(sibling),
        )

    def weight_rows(f):
        return every_weight.at[pl.ds(pl.multiple_of(f * BLOCK, BLOCK), BLOCK)]

    def weight_side(f, side):
        return every_weight.at[
            pl.ds(pl.multiple_of(f * BLOCK, BLOCK), BLOCK), pl.ds(side * SIDE, SIDE)
        ]

    def ring(u, k, f, side, to):
        send(weight_side(f, side), weight_side(f, side), row_send.at[u, k], row_recv.at[u, k], device(to))

    def share_weight(u, k, f):
        send(weight_rows(f), weight_rows(f), pair_send.at[u, k], pair_recv.at[u, k], device(sibling))

    column = (x, 1 - x)

    def ring_first(u):
        block = index(column[u], y, c)
        ring(u, 0, block, 0, up)
        ring(u, 1, block, 1, down)
        ring(u, 2, block, 1, up)
        ring(u, 3, block, 0, down)
        share_weight(u, 0, block)

    def ring_second(u):
        below, above = index(column[u], y - 1, c), index(column[u], y + 1, c)
        arrived(weight_side(below, 0), row_recv.at[u, 0])
        ring(u, 4, below, 0, up)
        arrived(weight_side(above, 1), row_recv.at[u, 1])
        ring(u, 5, above, 1, down)

    def share_near(u):
        below, above = index(column[u], y - 1, c), index(column[u], y + 1, c)
        arrived(weight_side(below, 1), row_recv.at[u, 2])
        share_weight(u, 1, below)
        arrived(weight_side(above, 0), row_recv.at[u, 3])
        share_weight(u, 2, above)

    def share_far(u):
        far = index(column[u], y + 2, c)
        arrived(weight_side(far, 0), row_recv.at[u, 4])
        arrived(weight_side(far, 1), row_recv.at[u, 5])
        share_weight(u, 3, far)

    def from_sibling(u, k):
        shift = (0, -1, 1, 2)[k]
        arrived(weight_rows(index(column[u], y + shift, 1 - c)), pair_recv.at[u, k])

    for j in range(2):
        send_grad(j)
    loads[0].wait()
    weight_rows(me)[...] = weights[...].astype(BF16)
    ring_first(0)
    send(weight_rows(me), weight_rows(me), pair_send.at[0, 4], pair_recv.at[0, 4], device(across))
    for j in range(2, CHUNKS):
        send_grad(j)

    for n in range(1, 6):
        loads[n].wait()
    fill_tables(keys, decay, strength, rows, cols)

    def quad_part(who, y_at):
        return core_quad.at[
            pl.ds(pl.multiple_of(y_at * HEAD, HEAD), HEAD), pl.ds(pl.multiple_of(who * SEQ, SEQ), SEQ)
        ]

    def head_copy(g, n):
        h = g * GROUP + n
        x_at, y_at, c_at = g // 2, (g % 2) * 2 + n // 2, n % 2
        mine = (x_at == x) & (c_at == c)
        item = copy(
            core_t.at[pl.ds(pl.multiple_of(h * HEAD, HEAD), HEAD)], quad_part(member, y_at),
            core_send.at[h], core_recv.at[member, y_at], device(index(x_at, y, c_at)),
        )
        return mine, y_at, item

    def heads(g, carry):
        results = delta_group(g, queries, keys, values, rows, cols)
        for n, result in enumerate(results):
            at = pl.ds(pl.multiple_of((g * GROUP + n) * HEAD, HEAD), HEAD)
            core[:, at] = result.astype(BF16)
            turned = result.T.astype(BF16)
            core_t[at, :] = turned
            mine, y_at, item = head_copy(g, n)

            @pl.when(mine)
            def _():
                quad_part(member, y_at)[...] = turned

            @pl.when(jnp.logical_not(mine))
            def _():
                item.start()

        return carry

    lax.fori_loop(0, GROUPS, heads, 0)

    def partial_at(shift, start, size):
        return partial.at[
            pl.ds(pl.multiple_of(lax.rem(y + shift + 4, 4) * BLOCK, BLOCK), BLOCK), pl.ds(start, size)
        ]

    def take_grad(j):
        arrived(grad_part(member_sibling, j), grad_recv.at[1, j])
        arrived(grad_part(member_corner, j), grad_recv.at[2, j])

    def partial_chunk(j):
        at = pl.ds(j * CHUNK, CHUNK)
        total = jnp.dot(core_quad[...], grad_quad[:, at], preferred_element_type=F32)
        partial[:, at] = (total * SCALE).astype(BF16)
        start, half = j * CHUNK, pl.ds(j * HALF, HALF)
        send(
            partial_at(2, start, HALF), relay_up.at[:, half],
            relay_send.at[0, j], relay_recv.at[0, j], device(up),
        )
        send(
            partial_at(2, start + HALF, HALF), relay_down.at[:, half],
            relay_send.at[1, j], relay_recv.at[1, j], device(down),
        )

    def relay_chunk(j):
        start, at, half = j * CHUNK, pl.ds(j * CHUNK, CHUNK), pl.ds(j * HALF, HALF)
        for shift, relay, k, place in ((1, relay_up, 0, start), (-1, relay_down, 1, start + HALF)):
            arrived(relay.at[:, half], relay_recv.at[k, j])
            spot = partial_at(shift, place, HALF)
            spot[...] = (spot[...].astype(F32) + relay[:, half].astype(F32)).astype(BF16)
        send(partial_at(1, start, CHUNK), sum_up.at[:, at], sum_send.at[0, j], sum_recv.at[0, j], device(up))
        send(partial_at(-1, start, CHUNK), sum_down.at[:, at], sum_send.at[1, j], sum_recv.at[1, j], device(down))

    power = jnp.full((1, 128), exponents[0, 0], jnp.int32).astype(F32)
    down_scale, up_scale = jnp.exp2(-power)[:, :1], jnp.exp2(power)[:, :1]

    def update_chunk(j):
        at = pl.ds(j * CHUNK, CHUNK)
        arrived(sum_up.at[:, at], sum_recv.at[0, j])
        arrived(sum_down.at[:, at], sum_recv.at[1, j])
        grad = partial_at(0, j * CHUNK, CHUNK)[...].astype(F32)
        grad = grad + sum_up[:, at].astype(F32) + sum_down[:, at].astype(F32)
        weight, base = weights[:, at], anchor[:, at]
        one = 0.9 * first[:, at] + 0.1 * grad
        two = 0.95 * second[:, at] + 0.05 * grad * grad
        updated = weight - 0.03 * (one / (jnp.sqrt(two) + 1e-08) + 0.1 * weight)
        encoded = jnp.clip((base - updated) * down_scale, -448.0, 448.0).astype(BF16)
        decoded[:, at] = (encoded.astype(F32) * up_scale).astype(BF16)
        if j % SENDS == SENDS - 1:
            group = j // SENDS
            span = pl.ds(group * SENDS * CHUNK, SENDS * CHUNK)
            for k, r in enumerate(others):
                send(
                    decoded.at[pl.ds(pl.multiple_of(r * SHARE, SHARE), SHARE), span],
                    shares.at[replica, :, span],
                    share_send.at[k, group], share_recv.at[replica, group],
                    {"replica": r, "fsdp": me},
                )

    for n in range(6, 11):
        loads[n].wait()
    ring_second(0)
    for yy in range(4):
        for who in (member_sibling, member_across, member_corner):
            arrived(quad_part(who, yy), core_recv.at[who, yy])

    for j in range(CHUNKS):
        pass_grad(j)
        if j >= 2:
            update_chunk(j - 2)
        if j >= 1:
            relay_chunk(j - 1)
        take_grad(j)
        partial_chunk(j)
        if j == 1:
            arrived(weight_rows(across), pair_recv.at[0, 4])
            ring_first(1)
        if j == 2:
            share_near(0)
        if j == 3:
            share_far(0)
    relay_chunk(CHUNKS - 1)
    update_chunk(CHUNKS - 2)
    ring_second(1)
    update_chunk(CHUNKS - 1)

    def outer_rows(r):
        return outer.at[pl.ds(pl.multiple_of(r * SHARE, SHARE), SHARE)]

    for group in range(CHUNKS // SENDS):
        span = pl.ds(group * SENDS * CHUNK, SENDS * CHUNK)
        for r in others:
            arrived(shares.at[r, :, span], share_recv.at[r, group])
    shares[replica] = decoded[pl.ds(pl.multiple_of(replica * SHARE, SHARE), SHARE), :]
    total = shares[0].astype(F32)
    for r in range(1, REPLICAS):
        total = total + shares[r].astype(F32)
    outer_rows(replica)[...] = (total * (1.0 / REPLICAS)).astype(BF16)
    for k, r in enumerate(others):
        send(
            outer_rows(replica), outer_rows(replica), outer_send.at[k], outer_recv.at[replica],
            {"replica": r, "fsdp": me},
        )

    def rows_of(x_at, y_at):
        return pl.multiple_of(x_at * 1024 + lax.rem(y_at + 4, 4) * 256, 256)

    def multiply(spots, size, begin, finish):
        def tile(n, carry):
            at = pl.ds(pl.multiple_of(n * CHUNK, CHUNK), CHUNK)
            total = None
            for spot in spots:
                term = jnp.dot(
                    core[:, pl.ds(spot, size)], every_weight[pl.ds(spot, size), at],
                    preferred_element_type=F32,
                )
                total = term if total is None else total + term
            if not begin:
                total = total + jnp.concatenate((first[:, at], second[:, at]), axis=0)
            if finish:
                partial[0:SEQ, at] = (total * SCALE).astype(BF16)
            else:
                first[:, at] = total[:BLOCK]
                second[:, at] = total[BLOCK:]
            return carry

        lax.fori_loop(0, CHUNKS, tile, 0)

    for k in range(4):
        from_sibling(0, k)
    multiply([pl.multiple_of(x * 1024, 1024)], 1024, True, False)
    share_near(1)

    def outer_step(r):
        spot = pl.ds(pl.multiple_of(r * SHARE, SHARE), SHARE)
        delta = outer[spot, :].astype(F32)
        moved = 0.9 * momentum[spot, :] + delta
        momentum[spot, :] = moved
        anchor[spot, :] = anchor[spot, :] - 0.7 * (delta + 0.9 * moved)

    outer_step(replica)
    for r in others:
        arrived(outer_rows(r), outer_recv.at[r])
        outer_step(r)
    stores = [
        pltpu.make_async_copy(anchor, new_anchor_hbm, store_sem.at[0]),
        pltpu.make_async_copy(momentum, new_momentum_hbm, store_sem.at[1]),
    ]
    for store in stores:
        store.start()

    for k in range(3):
        from_sibling(1, k)
    multiply([rows_of(1 - x, y + shift) for shift in (0, -1, 1)], 256, False, False)
    share_far(1)
    from_sibling(1, 3)
    for item in started:
        item.wait_send()
    multiply([rows_of(1 - x, y + 2)], 256, False, True)
    last = pltpu.make_async_copy(partial.at[0:SEQ], layer_out_hbm, store_sem.at[2])
    last.start()

    def finish_heads(g, carry):
        for n in range(GROUP):
            mine, _, item = head_copy(g, n)

            @pl.when(jnp.logical_not(mine))
            def _():
                item.wait_send()

        return carry

    lax.fori_loop(0, GROUPS, finish_heads, 0)
    for store in stores:
        store.wait()
    last.wait()


def on_device(
    queries, keys, values, log_decay, write_strength, out_grad, replica_weights,
    adam_first, adam_second, anchor, outer_momentum, exponents,
):
    dma = pltpu.SemaphoreType.DMA
    scratch = [
        pltpu.VMEM((SEQ, WIDTH), BF16),
        pltpu.VMEM((SEQ, WIDTH), BF16),
        pltpu.VMEM((SEQ, WIDTH), BF16),
        pltpu.VMEM((HEADS, SEQ), F32),
        pltpu.VMEM((HEADS, SEQ), F32),
        pltpu.VMEM((BLOCK, D), F32),
        pltpu.VMEM((BLOCK, D), F32),
        pltpu.VMEM((BLOCK, D), F32),
        pltpu.VMEM((BLOCK, D), F32),
        pltpu.VMEM((BLOCK, D), F32),
        pltpu.VMEM((GROUPS, 128, SEQ), F32),
        pltpu.VMEM((GROUPS, SEQ, 128), F32),
        pltpu.VMEM((SEQ, WIDTH), BF16),
        pltpu.VMEM((WIDTH, SEQ), BF16),
        pltpu.VMEM((4 * HEAD, 4 * SEQ), BF16),
        pltpu.VMEM((4 * SEQ, D), BF16),
        pltpu.VMEM((WIDTH, D), BF16),
        pltpu.VMEM((4 * BLOCK, D), BF16),
        pltpu.VMEM((BLOCK, SIDE), BF16),
        pltpu.VMEM((BLOCK, SIDE), BF16),
        pltpu.VMEM((BLOCK, D), BF16),
        pltpu.VMEM((BLOCK, D), BF16),
        pltpu.VMEM((BLOCK, D), BF16),
        pltpu.VMEM((REPLICAS, SHARE, D), BF16),
        pltpu.VMEM((BLOCK, D), BF16),
        dma((11,)), dma((3,)),
        dma((3, CHUNKS)), dma((3, CHUNKS)),
        dma((HEADS,)), dma((4, 4)),
        dma((2, 6)), dma((2, 6)),
        dma((2, 5)), dma((2, 5)),
        dma((2, CHUNKS)), dma((2, CHUNKS)),
        dma((2, CHUNKS)), dma((2, CHUNKS)),
        dma((REPLICAS - 1, CHUNKS // SENDS)), dma((REPLICAS, CHUNKS // SENDS)),
        dma((REPLICAS - 1,)), dma((REPLICAS,)),
    ]
    anywhere = pl.BlockSpec(memory_space=pl.ANY)
    return pl.pallas_call(
        kernel,
        out_shape=(
            jax.ShapeDtypeStruct((SEQ, D), BF16),
            jax.ShapeDtypeStruct((BLOCK, D), F32),
            jax.ShapeDtypeStruct((BLOCK, D), F32),
        ),
        in_specs=[anywhere] * 11 + [pl.BlockSpec(memory_space=pltpu.SMEM)],
        out_specs=(anywhere,) * 3,
        scratch_shapes=scratch,
        compiler_params=pltpu.CompilerParams(
            collective_id=0, has_side_effects=True, vmem_limit_bytes=60 * 1024 * 1024
        ),
        name="diloco_step",
    )(
        queries, keys, values, log_decay, write_strength, out_grad, replica_weights,
        adam_first, adam_second, anchor, outer_momentum, exponents,
    )


def solution(mesh):
    return jax.shard_map(
        on_device,
        mesh=mesh,
        in_specs=(
            P(("replica", "fsdp"), None),
            P(("replica", "fsdp"), None),
            P(("replica", "fsdp"), None),
            P(None, ("replica", "fsdp")),
            P(None, ("replica", "fsdp")),
            P(("replica", "fsdp"), None),
            P("replica", "fsdp", None),
            P("replica", "fsdp", None),
            P("replica", "fsdp", None),
            P("fsdp", None),
            P("fsdp", None),
            P("replica", "fsdp"),
        ),
        out_specs=(P(("replica", "fsdp"), None), P("fsdp", None), P("fsdp", None)),
        check_vma=False,
    )
```

time: 466 us -> 201 us (0.43)
  waiting for transfers between devices: 313 us -> 0 us
  Pallas kernels: 0 us -> 192 us
  matrix products: 86.5 us -> 0 us
  other arithmetic: 24.8 us -> 0 us
  blocking collectives: 16.1 us -> 0 us
  between operations: 15.3 us -> 1.3 us
    pallas_call x0 -> x1, Pallas kernels: none -> 192 us  [on_device(): pl.pallas_call(kernel, out_shape=(jax.ShapeDtypeStruct((SEQ, D), BF16), j...]
    all_gather x2 -> x0, waiting for transfers between devices: 167 us -> none  [the longest x1 87.1 us: on_device(): lax.all_gather(working, 'fsdp', axis=0, tiled=True)]
    reduce_scatter x1 -> x0, waiting for transfers between devices: 146 us -> none  [on_device(): lax.psum_scatter((term * scale).astype(jnp.bfloat16), 'fsdp', scatter_dim...]
    dot_general x24 -> x0, matrix products: 86.5 us -> none  [the longest x6 27.3 us: unit_lower_apply(): jnp.einsum('hnij,hnjc->hnic', power, result, precision=HIGH)]
    unnamed x1 -> x0, blocking collectives: 16.1 us -> none
    convert_element_type x3 -> x0, other arithmetic: 9.52 us -> none  [the longest x1 6.47 us: on_device(): jnp.clip(shaped * down_scale[:, None, None], -448.0, 448.0)]
    reduce_sum x2 -> x0, other arithmetic: 6.62 us -> none  [the longest x1 5.61 us: on_device(): total = jnp.sum(decoded, axis=0)]
  transfers between devices with their start and end apart: 3 -> 0, of which waited for: 3 -> 0; matrix products, arithmetic and copies ran while one was open for 5% -> 0% of each run, Pallas kernels for 0% -> 0%
where the time goes in v1:
time: 201 us
  Pallas kernels  192 us (96%)
  local copies, waits for them, and re-layouts  6.95 us (3%)
    pallas_call x1, Pallas kernels, on_device(): pl.pallas_call(kernel, out_shape=(jax.ShapeDtypeStruct((SEQ, D), BF16), j...  192 us
    unnamed x7, local copies, waits for them, and re-layouts  6.95 us

profile of v1, /device:TPU:1, one launch (start us, length us, event | category | flops | bytes accessed | tf_op | source)
XLA Modules:
  0.0 200.6 jit_solution(6749806315873220853)
XLA Ops:
  1.3 192.4 %diloco_step.1 = (bf16[256,4096]{1,0:T(8,128)(2,1)}, f32[128,4096]{1,0:T(8,128)}, f32[128,4096]{1,0:T(8,128)}) custom-call(bf16[256,2048]{1,0:T(8,128)(2,1)} %queries_hbm.1, bf16[256,2048]{1,0:T(8,128)(2,1)} %keys_hbm.1, bf16[256,2048]{1,0:T(8,128)(2,1)} %values_hbm.1, f32[16,256]{1,0:T(8,128)} %decay_hbm.1, f32[16,256]{1,0:T(8,128)} %strength_hbm.1, ...), custom_call_target="tpu_custom_call" | custom-call | tf_op jit(solution)/shard_map/diloco_step/pallas_call | solution.py:523
  193.7 0.0 copy-start.1
  193.7 3.3 %copy.19 = bf16[256,4096]{1,0:T(8,128)(2,1)} copy(bf16[256,4096]{1,0:T(8,128)(2,1)} %get-tuple-element.6) | data formatting | bytes 4194304
  197.0 0.0 copy-done.1
  197.0 0.0 copy-start
  197.0 1.3 copy.20
  198.3 1.0 copy-done
  199.3 1.3 copy.21
Async XLA Ops:
  193.7 3.3 %copy-start.1 = (f32[128,4096]{1,0:T(8,128)S(1)}, f32[128,4096]{1,0:T(8,128)}, u32[]{:S(2)}) copy-start(f32[128,4096]{1,0:T(8,128)} %get-tuple-element.7) | copy-start | bytes 6291460
  197.0 2.3 %copy-start = (f32[128,4096]{1,0:T(8,128)S(1)}, f32[128,4096]{1,0:T(8,128)}, u32[]{:S(2)}) copy-start(f32[128,4096]{1,0:T(8,128)} %get-tuple-element.8) | copy-start | bytes 6291460

commit v2 on v1

--- a/solution.py
+++ b/solution.py
@@ -12,15 +12,18 @@
 D = 4096
 BLOCK = 128
 REPLICAS = 8
-SHARE = BLOCK // REPLICAS
+SHARE = BLOCK // 4
 GROUP = 4
 GROUPS = HEADS // GROUP
 CHUNK = 512
 CHUNKS = D // CHUNK
 HALF = CHUNK // 2
 SIDE = D // 2
+QUARTER = D // 4
+EARLY = 2
 SCALE = WIDTH ** (-0.5)
 SENDS = 2
+SPAN = SENDS * CHUNK
 F32 = jnp.float32
 BF16 = jnp.bfloat16
 NT = (((1,), (1,)), ((), ()))
@@ -133,11 +136,11 @@
     first_hbm, second_hbm, anchor_hbm, momentum_hbm, exponents,
     layer_out_hbm, new_anchor_hbm, new_momentum_hbm,
     queries, keys, values, decay, strength, weights, first, second, anchor, momentum,
-    rows, cols, core, core_t, core_quad, grad_quad, every_weight, partial,
-    relay_up, relay_down, sum_up, sum_down, decoded, shares, outer,
-    load_sem, store_sem, grad_send, grad_recv, core_send, core_recv, row_send, row_recv,
-    pair_send, pair_recv, relay_send, relay_recv, sum_send, sum_recv,
-    share_send, share_recv, outer_send, outer_recv,
+    rows, cols, core, core_t, across_t, across_n, out_sent, out_across, core_quad, grad_quad, every_weight, partial,
+    relay_up, relay_down, sum_up, sum_down, decoded, shares, halves, outer,
+    load_sem, store_sem, grad_send, grad_recv, quad_send, quad_recv, row_send, row_recv,
+    pair_send, pair_recv, cross_send, cross_recv, out_send, out_recv, relay_send, relay_recv, sum_send, sum_recv,
+    share_send, share_recv, half_send, half_recv, outer_send, outer_recv,
 ):
     replica, me = lax.axis_index("replica"), lax.axis_index("fsdp")
     x, y, c = me // 8, (me // 2) % 4, me % 2
@@ -150,11 +153,17 @@
 
     sibling, across, corner = index(x, y, 1 - c), index(1 - x, y, c), index(1 - x, y, 1 - c)
     up, down = index(x, y + 1, c), index(x, y - 1, c)
-    others = [lax.rem(replica + k, REPLICAS) for k in range(1, REPLICAS)]
+    z = lax.rem(replica, 4)
+    half = replica // 4
+    others = [lax.rem(z + k, 4) for k in range(1, 4)]
+
+    def replica_at(half_at, z_at):
+        return {"replica": half_at * 4 + z_at, "fsdp": me}
+
     member = x * 2 + c
     member_sibling, member_across, member_corner = x * 2 + 1 - c, (1 - x) * 2 + c, (1 - x) * 2 + 1 - c
 
-    started = []
+    started, late = [], []
 
     def copy(src, dst, send_sem, recv_sem, to):
         return pltpu.make_async_remote_copy(
@@ -162,10 +171,10 @@
             device_id=to, device_id_type=MESH,
         )
 
-    def send(src, dst, send_sem, recv_sem, to):
+    def send(src, dst, send_sem, recv_sem, to, kept=started):
         item = copy(src, dst, send_sem, recv_sem, to)
         item.start()
-        started.append(item)
+        kept.append(item)
 
     def arrived(region, recv_sem):
         copy(region, region, recv_sem, recv_sem, device(sibling)).wait_recv()
@@ -177,15 +186,18 @@
         (second_hbm.at[0], second), (anchor_hbm, anchor), (momentum_hbm, momentum),
     ]
     loads = [pltpu.make_async_copy(src, dst, load_sem.at[n]) for n, (src, dst) in enumerate(loads)]
-    for load in loads:
+    for load in loads[:6]:
         load.start()
 
     barrier = pltpu.get_barrier_semaphore()
     peers = [device(f) for f in (sibling, across, corner, up, down)]
-    peers += [{"replica": r, "fsdp": me} for r in others]
+    peers += [replica_at(half, zz) for zz in others] + [replica_at(1 - half, z)]
     for peer in peers:
         pl.semaphore_signal(barrier, inc=1, device_id=peer, device_id_type=MESH)
     pl.semaphore_wait(barrier, len(peers))
+
+    def weight_rows(f):
+        return every_weight.at[pl.ds(pl.multiple_of(f * BLOCK, BLOCK), BLOCK)]
 
     def grad_part(who, j):
         return grad_quad.at[
@@ -204,102 +216,112 @@
             grad_send.at[2, j], grad_recv.at[2, j], device(sibling),
         )
 
-    def weight_rows(f):
-        return every_weight.at[pl.ds(pl.multiple_of(f * BLOCK, BLOCK), BLOCK)]
+    def weight_part(f, start, size):
+        return every_weight.at[
+            pl.ds(pl.multiple_of(f * BLOCK, BLOCK), BLOCK), pl.ds(start, size)
+        ]
 
     def weight_side(f, side):
-        return every_weight.at[
-            pl.ds(pl.multiple_of(f * BLOCK, BLOCK), BLOCK), pl.ds(side * SIDE, SIDE)
-        ]
-
-    def ring(u, k, f, side, to):
-        send(weight_side(f, side), weight_side(f, side), row_send.at[u, k], row_recv.at[u, k], device(to))
-
-    def share_weight(u, k, f):
-        send(weight_rows(f), weight_rows(f), pair_send.at[u, k], pair_recv.at[u, k], device(sibling))
+        return weight_part(f, side * SIDE, SIDE)
+
+    def ring(u, side, k, f, half, to):
+        part = weight_part(f, side * SIDE + half * QUARTER, QUARTER)
+        send(part, part, row_send.at[u, side, k], row_recv.at[u, side, k], device(to), (started, late)[u])
+
+    def ring_arrived(u, side, k, f, half):
+        arrived(weight_part(f, side * SIDE + half * QUARTER, QUARTER), row_recv.at[u, side, k])
+
+    def share_weight(u, side, k, f):
+        part = weight_side(f, side)
+        send(
+            part, part, pair_send.at[u, side, k], pair_recv.at[u, side, k], device(sibling), (started, late)[u]
+        )
 
     column = (x, 1 - x)
 
-    def ring_first(u):
+    def ring_first(u, side, step):
         block = index(column[u], y, c)
-        ring(u, 0, block, 0, up)
-        ring(u, 1, block, 1, down)
-        ring(u, 2, block, 1, up)
-        ring(u, 3, block, 0, down)
-        share_weight(u, 0, block)
-
-    def ring_second(u):
+        ring(u, side, 2 * step, block, step, up)
+        ring(u, side, 2 * step + 1, block, 1 - step, down)
+
+    def ring_second(u, side):
         below, above = index(column[u], y - 1, c), index(column[u], y + 1, c)
-        arrived(weight_side(below, 0), row_recv.at[u, 0])
-        ring(u, 4, below, 0, up)
-        arrived(weight_side(above, 1), row_recv.at[u, 1])
-        ring(u, 5, above, 1, down)
-
-    def share_near(u):
+        ring_arrived(u, side, 0, below, 0)
+        ring(u, side, 4, below, 0, up)
+        ring_arrived(u, side, 1, above, 1)
+        ring(u, side, 5, above, 1, down)
+
+    def share_near(u, side):
         below, above = index(column[u], y - 1, c), index(column[u], y + 1, c)
-        arrived(weight_side(below, 1), row_recv.at[u, 2])
-        share_weight(u, 1, below)
-        arrived(weight_side(above, 0), row_recv.at[u, 3])
-        share_weight(u, 2, above)
-
-    def share_far(u):
+        ring_arrived(u, side, 2, below, 1)
+        share_weight(u, side, 1, below)
+        ring_arrived(u, side, 3, above, 0)
+        share_weight(u, side, 2, above)
+
+    def share_far(u, side):
         far = index(column[u], y + 2, c)
-        arrived(weight_side(far, 0), row_recv.at[u, 4])
-        arrived(weight_side(far, 1), row_recv.at[u, 5])
-        share_weight(u, 3, far)
-
-    def from_sibling(u, k):
+        ring_arrived(u, side, 4, far, 0)
+        ring_arrived(u, side, 5, far, 1)
+        share_weight(u, side, 3, far)
+
+    def from_sibling(u, side, k):
         shift = (0, -1, 1, 2)[k]
-        arrived(weight_rows(index(column[u], y + shift, 1 - c)), pair_recv.at[u, k])
-
-    for j in range(2):
+        arrived(weight_side(index(column[u], y + shift, 1 - c), side), pair_recv.at[u, side, k])
+
+    for j in range(EARLY):
         send_grad(j)
     loads[0].wait()
     weight_rows(me)[...] = weights[...].astype(BF16)
-    ring_first(0)
-    send(weight_rows(me), weight_rows(me), pair_send.at[0, 4], pair_recv.at[0, 4], device(across))
-    for j in range(2, CHUNKS):
-        send_grad(j)
+    for side in range(2):
+        ring_first(0, side, 0)
+        ring_first(0, side, 1)
+    for side in range(2):
+        share_weight(0, side, 0, me)
+    for load in loads[6:]:
+        load.start()
 
     for n in range(1, 6):
         loads[n].wait()
     fill_tables(keys, decay, strength, rows, cols)
-
-    def quad_part(who, y_at):
-        return core_quad.at[
-            pl.ds(pl.multiple_of(y_at * HEAD, HEAD), HEAD), pl.ds(pl.multiple_of(who * SEQ, SEQ), SEQ)
-        ]
-
-    def head_copy(g, n):
-        h = g * GROUP + n
-        x_at, y_at, c_at = g // 2, (g % 2) * 2 + n // 2, n % 2
-        mine = (x_at == x) & (c_at == c)
-        item = copy(
-            core_t.at[pl.ds(pl.multiple_of(h * HEAD, HEAD), HEAD)], quad_part(member, y_at),
-            core_send.at[h], core_recv.at[member, y_at], device(index(x_at, y, c_at)),
-        )
-        return mine, y_at, item
 
     def heads(g, carry):
         results = delta_group(g, queries, keys, values, rows, cols)
         for n, result in enumerate(results):
             at = pl.ds(pl.multiple_of((g * GROUP + n) * HEAD, HEAD), HEAD)
             core[:, at] = result.astype(BF16)
-            turned = result.T.astype(BF16)
-            core_t[at, :] = turned
-            mine, y_at, item = head_copy(g, n)
-
-            @pl.when(mine)
-            def _():
-                quad_part(member, y_at)[...] = turned
-
-            @pl.when(jnp.logical_not(mine))
-            def _():
-                item.start()
-
+            core_t[at, :] = result.T.astype(BF16)
         return carry
 
-    lax.fori_loop(0, GROUPS, heads, 0)
+    lax.fori_loop((1 - x) * 2, (1 - x) * 2 + 2, heads, 0)
+    ring_second(0, 0)
+    other_rows = core_t.at[pl.ds(pl.multiple_of((1 - x) * 1024, 1024), 1024)]
+    send(other_rows, across_t, cross_send.at[0], cross_recv.at[0], device(across))
+    for j in range(EARLY, CHUNKS):
+        send_grad(j)
+    part = weight_side(me, 0)
+    send(part, part, cross_send.at[1], cross_recv.at[1], device(across))
+    lax.fori_loop(x * 2, x * 2 + 2, heads, 0)
+    ring_second(0, 1)
+
+    def quad_part(who, y_at):
+        return core_quad.at[
+            pl.ds(pl.multiple_of(y_at * HEAD, HEAD), HEAD), pl.ds(pl.multiple_of(who * SEQ, SEQ), SEQ)
+        ]
+
+    def head_rows(ref, h):
+        return ref.at[pl.ds(pl.multiple_of(h * HEAD, HEAD), HEAD)]
+
+    def hand_out(k, ref, base, who):
+        for yy in range(4):
+            send(
+                head_rows(ref, base + 2 * yy + 1 - c), quad_part(who, yy),
+                quad_send.at[k, yy], quad_recv.at[k, yy], device(sibling),
+            )
+            quad_part(who, yy)[...] = head_rows(ref, base + 2 * yy + c)[...]
+
+    hand_out(0, core_t, x * 8, member)
+    arrived(across_t, cross_recv.at[0])
+    hand_out(1, across_t, 0, member_across)
 
     def partial_at(shift, start, size):
         return partial.at[
@@ -350,64 +372,106 @@
         decoded[:, at] = (encoded.astype(F32) * up_scale).astype(BF16)
         if j % SENDS == SENDS - 1:
             group = j // SENDS
-            span = pl.ds(group * SENDS * CHUNK, SENDS * CHUNK)
-            for k, r in enumerate(others):
+            span = pl.ds(group * SPAN, SPAN)
+            for k, zz in enumerate(others):
                 send(
-                    decoded.at[pl.ds(pl.multiple_of(r * SHARE, SHARE), SHARE), span],
-                    shares.at[replica, :, span],
-                    share_send.at[k, group], share_recv.at[replica, group],
-                    {"replica": r, "fsdp": me},
+                    decoded.at[pl.ds(pl.multiple_of(zz * SHARE, SHARE), SHARE), span], shares.at[z, :, span],
+                    share_send.at[k, group], share_recv.at[z, group], replica_at(half, zz),
                 )
 
+    def share_rows(zz):
+        return pl.ds(pl.multiple_of(zz * SHARE, SHARE), SHARE)
+
+    def share_group(group):
+        span = pl.ds(group * SPAN, SPAN)
+        for zz in others:
+            arrived(shares.at[zz, :, span], share_recv.at[zz, group])
+        shares[z, :, span] = decoded[share_rows(z), span]
+        total = shares[0, :, span].astype(F32)
+        for zz in range(1, 4):
+            total = total + shares[zz, :, span].astype(F32)
+        halves[half, :, span] = total.astype(BF16)
+        send(
+            halves.at[half, :, span], halves.at[half, :, span],
+            half_send.at[group], half_recv.at[group], replica_at(1 - half, z),
+        )
+
+    def outer_group(group):
+        span = pl.ds(group * SPAN, SPAN)
+        arrived(halves.at[1 - half, :, span], half_recv.at[group])
+        total = halves[0, :, span].astype(F32) + halves[1, :, span].astype(F32)
+        outer[share_rows(z), span] = (total * (1.0 / REPLICAS)).astype(BF16)
+        part = outer.at[share_rows(z), span]
+        for k, zz in enumerate(others):
+            send(part, part, outer_send.at[k, group], outer_recv.at[z, group], replica_at(half, zz), late)
+
+    def product_across():
+        for h in range(8):
+            across_n[:, h * HEAD : (h + 1) * HEAD] = (
+                across_t[h * HEAD : (h + 1) * HEAD, :].astype(F32).T.astype(BF16)
+            )
+
+        def tile(n, carry):
+            at = pl.multiple_of(n * CHUNK, CHUNK)
+            total = jnp.dot(
+                across_n[...],
+                every_weight[pl.ds(pl.multiple_of(x * 1024, 1024), 1024), pl.ds(SIDE + at, CHUNK)],
+                preferred_element_type=F32,
+            )
+            out_sent[:, pl.ds(at, CHUNK)] = (total * SCALE).astype(BF16)
+            return carry
+
+        lax.fori_loop(0, SIDE // CHUNK, tile, 0)
+
+    def send_product(k):
+        at = pl.ds(k * CHUNK, CHUNK)
+        send(out_sent.at[:, at], out_across.at[:, at], out_send.at[k], out_recv.at[k], device(across), late)
+
+    for j in range(EARLY):
+        pass_grad(j)
     for n in range(6, 11):
         loads[n].wait()
-    ring_second(0)
     for yy in range(4):
-        for who in (member_sibling, member_across, member_corner):
-            arrived(quad_part(who, yy), core_recv.at[who, yy])
+        arrived(quad_part(member_sibling, yy), quad_recv.at[0, yy])
+        arrived(quad_part(member_corner, yy), quad_recv.at[1, yy])
 
     for j in range(CHUNKS):
-        pass_grad(j)
+        take_grad(j)
+        partial_chunk(j)
         if j >= 2:
             update_chunk(j - 2)
         if j >= 1:
             relay_chunk(j - 1)
-        take_grad(j)
-        partial_chunk(j)
-        if j == 1:
-            arrived(weight_rows(across), pair_recv.at[0, 4])
-            ring_first(1)
+        if EARLY <= j + 1 < CHUNKS:
+            pass_grad(j + 1)
         if j == 2:
-            share_near(0)
+            share_near(0, 0)
+            share_near(0, 1)
         if j == 3:
-            share_far(0)
+            share_far(0, 0)
+            share_far(0, 1)
+        if j == 4:
+            for k in range(4):
+                from_sibling(0, 1, k)
+            product_across()
+            send_product(0)
+        if j >= 6:
+            share_group(j - 6)
     relay_chunk(CHUNKS - 1)
     update_chunk(CHUNKS - 2)
-    ring_second(1)
+    share_group(2)
     update_chunk(CHUNKS - 1)
-
-    def outer_rows(r):
-        return outer.at[pl.ds(pl.multiple_of(r * SHARE, SHARE), SHARE)]
-
-    for group in range(CHUNKS // SENDS):
-        span = pl.ds(group * SENDS * CHUNK, SENDS * CHUNK)
-        for r in others:
-            arrived(shares.at[r, :, span], share_recv.at[r, group])
-    shares[replica] = decoded[pl.ds(pl.multiple_of(replica * SHARE, SHARE), SHARE), :]
-    total = shares[0].astype(F32)
-    for r in range(1, REPLICAS):
-        total = total + shares[r].astype(F32)
-    outer_rows(replica)[...] = (total * (1.0 / REPLICAS)).astype(BF16)
-    for k, r in enumerate(others):
-        send(
-            outer_rows(replica), outer_rows(replica), outer_send.at[k], outer_recv.at[replica],
-            {"replica": r, "fsdp": me},
-        )
-
-    def rows_of(x_at, y_at):
-        return pl.multiple_of(x_at * 1024 + lax.rem(y_at + 4, 4) * 256, 256)
-
-    def multiply(spots, size, begin, finish):
+    arrived(weight_side(across, 0), cross_recv.at[1])
+    ring_first(1, 0, 0)
+    ring_first(1, 0, 1)
+    share_weight(1, 0, 0, across)
+    share_group(3)
+    for k in range(1, SIDE // CHUNK):
+        send_product(k)
+    for group in range(3):
+        outer_group(group)
+
+    def multiply(tiles, spots, size, begin, finish):
         def tile(n, carry):
             at = pl.ds(pl.multiple_of(n * CHUNK, CHUNK), CHUNK)
             total = None
@@ -426,24 +490,32 @@
                 second[:, at] = total[BLOCK:]
             return carry
 
-        lax.fori_loop(0, CHUNKS, tile, 0)
+        lax.fori_loop(tiles[0], tiles[1], tile, 0)
+
+    def store_out(k):
+        at = pl.ds(0, SIDE) if k == 0 else pl.ds(SIDE + (k - 1) * CHUNK, CHUNK)
+        return pltpu.make_async_copy(partial.at[0:SEQ, at], layer_out_hbm.at[:, at], store_sem.at[2 + k])
 
     for k in range(4):
-        from_sibling(0, k)
-    multiply([pl.multiple_of(x * 1024, 1024)], 1024, True, False)
-    share_near(1)
-
-    def outer_step(r):
-        spot = pl.ds(pl.multiple_of(r * SHARE, SHARE), SHARE)
+        from_sibling(0, 0, k)
+    multiply((0, CHUNKS), [pl.multiple_of(x * 1024, 1024)], 1024, True, False)
+    outer_group(3)
+    ring_second(1, 0)
+    for item in started:
+        item.wait_send()
+
+    def outer_step(zz):
+        spot = share_rows(zz)
         delta = outer[spot, :].astype(F32)
         moved = 0.9 * momentum[spot, :] + delta
         momentum[spot, :] = moved
         anchor[spot, :] = anchor[spot, :] - 0.7 * (delta + 0.9 * moved)
 
-    outer_step(replica)
-    for r in others:
-        arrived(outer_rows(r), outer_recv.at[r])
-        outer_step(r)
+    outer_step(z)
+    for zz in others:
+        for group in range(CHUNKS // SENDS):
+            arrived(outer.at[share_rows(zz), pl.ds(group * SPAN, SPAN)], outer_recv.at[zz, group])
+        outer_step(zz)
     stores = [
         pltpu.make_async_copy(anchor, new_anchor_hbm, store_sem.at[0]),
         pltpu.make_async_copy(momentum, new_momentum_hbm, store_sem.at[1]),
@@ -451,31 +523,25 @@
     for store in stores:
         store.start()
 
-    for k in range(3):
-        from_sibling(1, k)
-    multiply([rows_of(1 - x, y + shift) for shift in (0, -1, 1)], 256, False, False)
-    share_far(1)
-    from_sibling(1, 3)
-    for item in started:
+    share_near(1, 0)
+    share_far(1, 0)
+    for k in range(4):
+        from_sibling(1, 0, k)
+    multiply((0, CHUNKS // 2), [pl.multiple_of((1 - x) * 1024, 1024)], 1024, False, True)
+    outs = [store_out(k) for k in range(5)]
+    outs[0].start()
+    for k in range(SIDE // CHUNK):
+        part, at = pl.ds(k * CHUNK, CHUNK), pl.ds(SIDE + k * CHUNK, CHUNK)
+        arrived(out_across.at[:, part], out_recv.at[k])
+        for ref, spot in ((first, pl.ds(0, BLOCK)), (second, pl.ds(BLOCK, BLOCK))):
+            partial[spot, at] = (ref[:, at] * SCALE + out_across[spot, part].astype(F32)).astype(BF16)
+        outs[k + 1].start()
+    for item in late:
         item.wait_send()
-    multiply([rows_of(1 - x, y + 2)], 256, False, True)
-    last = pltpu.make_async_copy(partial.at[0:SEQ], layer_out_hbm, store_sem.at[2])
-    last.start()
-
-    def finish_heads(g, carry):
-        for n in range(GROUP):
-            mine, _, item = head_copy(g, n)
-
-            @pl.when(jnp.logical_not(mine))
-            def _():
-                item.wait_send()
-
-        return carry
-
-    lax.fori_loop(0, GROUPS, finish_heads, 0)
     for store in stores:
         store.wait()
-    last.wait()
+    for out in outs:
+        out.wait()
 
 
 def on_device(
@@ -498,6 +564,10 @@
         pltpu.VMEM((GROUPS, SEQ, 128), F32),
         pltpu.VMEM((SEQ, WIDTH), BF16),
         pltpu.VMEM((WIDTH, SEQ), BF16),
+        pltpu.VMEM((WIDTH // 2, SEQ), BF16),
+        pltpu.VMEM((SEQ, WIDTH // 2), BF16),
+        pltpu.VMEM((SEQ, SIDE), BF16),
+        pltpu.VMEM((SEQ, SIDE), BF16),
         pltpu.VMEM((4 * HEAD, 4 * SEQ), BF16),
         pltpu.VMEM((4 * SEQ, D), BF16),
         pltpu.VMEM((WIDTH, D), BF16),
@@ -507,17 +577,21 @@
         pltpu.VMEM((BLOCK, D), BF16),
         pltpu.VMEM((BLOCK, D), BF16),
         pltpu.VMEM((BLOCK, D), BF16),
-        pltpu.VMEM((REPLICAS, SHARE, D), BF16),
+        pltpu.VMEM((4, SHARE, D), BF16),
+        pltpu.VMEM((2, SHARE, D), BF16),
         pltpu.VMEM((BLOCK, D), BF16),
-        dma((11,)), dma((3,)),
+        dma((11,)), dma((7,)),
         dma((3, CHUNKS)), dma((3, CHUNKS)),
-        dma((HEADS,)), dma((4, 4)),
-        dma((2, 6)), dma((2, 6)),
-        dma((2, 5)), dma((2, 5)),
+        dma((2, 4)), dma((2, 4)),
+        dma((2, 2, 6)), dma((2, 2, 6)),
+        dma((2, 2, 4)), dma((2, 2, 4)),
+        dma((2,)), dma((2,)),
+        dma((4,)), dma((4,)),
         dma((2, CHUNKS)), dma((2, CHUNKS)),
         dma((2, CHUNKS)), dma((2, CHUNKS)),
-        dma((REPLICAS - 1, CHUNKS // SENDS)), dma((REPLICAS, CHUNKS // SENDS)),
-        dma((REPLICAS - 1,)), dma((REPLICAS,)),
+        dma((3, 4)), dma((4, 4)),
+        dma((4,)), dma((4,)),
+        dma((3, 4)), dma((4, 4)),
     ]
     anywhere = pl.BlockSpec(memory_space=pl.ANY)
     return pl.pallas_call(

time: 201 us -> 118 us (0.59)
  Pallas kernels: 192 us -> 109 us
    pallas_call x1, Pallas kernels: 192 us -> 109 us  [on_device(): pl.pallas_call(kernel, out_shape=(jax.ShapeDtypeStruct((SEQ, D), BF16), j...]
where the time goes in v2:
time: 118 us; the launch traced here: 117 us
  Pallas kernels  109 us (92%)
  local copies, waits for them, and re-layouts  6.95 us (6%)
  between operations  1.3 us (1%)
    pallas_call x1, Pallas kernels, on_device(): pl.pallas_call(kernel, out_shape=(jax.ShapeDtypeStruct((SEQ, D), BF16), j...  109 us
    unnamed x7, local copies, waits for them, and re-layouts  6.95 us

profile of v2, /device:TPU:1, one launch (start us, length us, event | category | flops | bytes accessed | tf_op | source)
XLA Modules:
  0.0 117.5 jit_solution(7293279549168542814)
XLA Ops:
  1.3 109.2 %diloco_step.1 = (bf16[256,4096]{1,0:T(8,128)(2,1)}, f32[128,4096]{1,0:T(8,128)}, f32[128,4096]{1,0:T(8,128)}) custom-call(bf16[256,2048]{1,0:T(8,128)(2,1)} %queries_hbm.1, bf16[256,2048]{1,0:T(8,128)(2,1)} %keys_hbm.1, bf16[256,2048]{1,0:T(8,128)(2,1)} %values_hbm.1, f32[16,256]{1,0:T(8,128)} %decay_hbm.1, f32[16,256]{1,0:T(8,128)} %strength_hbm.1, ...), custom_call_target="tpu_custom_call" | custom-call | tf_op jit(solution)/shard_map/diloco_step/pallas_call | solution.py:597
  110.5 0.0 copy-start.1
  110.5 3.3 %copy.19 = bf16[256,4096]{1,0:T(8,128)(2,1)} copy(bf16[256,4096]{1,0:T(8,128)(2,1)} %get-tuple-element.6) | data formatting | bytes 4194304
  113.8 0.0 copy-done.1
  113.8 0.0 copy-start
  113.8 1.3 %copy.20 = f32[128,4096]{1,0:T(8,128)} copy(f32[128,4096]{1,0:T(8,128)S(1)} %copy-done.1) | data formatting | bytes 4194304
  115.1 1.0 copy-done
  116.1 1.3 %copy.21 = f32[128,4096]{1,0:T(8,128)} copy(f32[128,4096]{1,0:T(8,128)S(1)} %copy-done) | data formatting | bytes 4194304
Async XLA Ops:
  110.5 3.3 %copy-start.1 = (f32[128,4096]{1,0:T(8,128)S(1)}, f32[128,4096]{1,0:T(8,128)}, u32[]{:S(2)}) copy-start(f32[128,4096]{1,0:T(8,128)} %get-tuple-element.7) | copy-start | bytes 6291460
  113.8 2.3 %copy-start = (f32[128,4096]{1,0:T(8,128)S(1)}, f32[128,4096]{1,0:T(8,128)}, u32[]{:S(2)}) copy-start(f32[128,4096]{1,0:T(8,128)} %get-tuple-element.8) | copy-start | bytes 6291460

commit v3 on v2

--- a/solution.py
+++ b/solution.py
@@ -19,9 +19,13 @@
 CHUNKS = D // CHUNK
 HALF = CHUNK // 2
 SIDE = D // 2
-QUARTER = D // 4
+PIECES = (((0, 2048), (2048, 2048)), ((0, 2048),))
+WHOLE = 2048
+SHARED = D - WHOLE
+TILE = 512
+OUTS = ((0, 2048), (2048, 512), (2560, 512), (3072, 512), (3584, 512))
+SCALE = WIDTH ** (-0.5)
 EARLY = 2
-SCALE = WIDTH ** (-0.5)
 SENDS = 2
 SPAN = SENDS * CHUNK
 F32 = jnp.float32
@@ -134,7 +138,7 @@
 def kernel(
     queries_hbm, keys_hbm, values_hbm, decay_hbm, strength_hbm, out_grad_hbm, weights_hbm,
     first_hbm, second_hbm, anchor_hbm, momentum_hbm, exponents,
-    layer_out_hbm, new_anchor_hbm, new_momentum_hbm,
+    layer_out_hbm, state_hbm,
     queries, keys, values, decay, strength, weights, first, second, anchor, momentum,
     rows, cols, core, core_t, across_t, across_n, out_sent, out_across, core_quad, grad_quad, every_weight, partial,
     relay_up, relay_down, sum_up, sum_down, decoded, shares, halves, outer,
@@ -186,14 +190,13 @@
         (second_hbm.at[0], second), (anchor_hbm, anchor), (momentum_hbm, momentum),
     ]
     loads = [pltpu.make_async_copy(src, dst, load_sem.at[n]) for n, (src, dst) in enumerate(loads)]
-    for load in loads[:6]:
-        load.start()
-
     barrier = pltpu.get_barrier_semaphore()
     peers = [device(f) for f in (sibling, across, corner, up, down)]
     peers += [replica_at(half, zz) for zz in others] + [replica_at(1 - half, z)]
     for peer in peers:
         pl.semaphore_signal(barrier, inc=1, device_id=peer, device_id_type=MESH)
+    for load in loads[:6]:
+        load.start()
     pl.semaphore_wait(barrier, len(peers))
 
     def weight_rows(f):
@@ -221,62 +224,75 @@
             pl.ds(pl.multiple_of(f * BLOCK, BLOCK), BLOCK), pl.ds(start, size)
         ]
 
-    def weight_side(f, side):
-        return weight_part(f, side * SIDE, SIDE)
-
-    def ring(u, side, k, f, half, to):
-        part = weight_part(f, side * SIDE + half * QUARTER, QUARTER)
-        send(part, part, row_send.at[u, side, k], row_recv.at[u, side, k], device(to), (started, late)[u])
-
-    def ring_arrived(u, side, k, f, half):
-        arrived(weight_part(f, side * SIDE + half * QUARTER, QUARTER), row_recv.at[u, side, k])
-
-    def share_weight(u, side, k, f):
-        part = weight_side(f, side)
-        send(
-            part, part, pair_send.at[u, side, k], pair_recv.at[u, side, k], device(sibling), (started, late)[u]
-        )
+    def weight_piece(u, p, f):
+        return weight_part(f, *PIECES[u][p])
+
+    def weight_half(u, p, f, side):
+        start, size = PIECES[u][p]
+        return weight_part(f, start + side * size // 2, size // 2)
+
+    def ring(u, p, k, f, side, to):
+        part = weight_half(u, p, f, side)
+        send(part, part, row_send.at[u, p, k], row_recv.at[u, p, k], device(to), (started, late)[u])
+
+    def ring_arrived(u, p, k, f, side):
+        arrived(weight_half(u, p, f, side), row_recv.at[u, p, k])
+
+    def share_weight(u, p, k, f):
+        part = weight_piece(u, p, f)
+        send(part, part, pair_send.at[u, p, k], pair_recv.at[u, p, k], device(sibling), (started, late)[u])
+
+    def cross_weight(p):
+        part = weight_piece(1, p, me)
+        send(part, part, cross_send.at[1 + p], cross_recv.at[1 + p], device(across))
+
+    def take_weight(p):
+        arrived(weight_piece(1, p, across), cross_recv.at[1 + p])
+        ring_first(1, p, 0)
+        ring_first(1, p, 1)
+        share_weight(1, p, 0, across)
 
     column = (x, 1 - x)
 
-    def ring_first(u, side, step):
+    def ring_first(u, p, step):
         block = index(column[u], y, c)
-        ring(u, side, 2 * step, block, step, up)
-        ring(u, side, 2 * step + 1, block, 1 - step, down)
-
-    def ring_second(u, side):
+        ring(u, p, 2 * step, block, step, up)
+        ring(u, p, 2 * step + 1, block, 1 - step, down)
+
+    def ring_second(u, p):
         below, above = index(column[u], y - 1, c), index(column[u], y + 1, c)
-        ring_arrived(u, side, 0, below, 0)
-        ring(u, side, 4, below, 0, up)
-        ring_arrived(u, side, 1, above, 1)
-        ring(u, side, 5, above, 1, down)
-
-    def share_near(u, side):
+        ring_arrived(u, p, 0, below, 0)
+        ring(u, p, 4, below, 0, up)
+        ring_arrived(u, p, 1, above, 1)
+        ring(u, p, 5, above, 1, down)
+
+    def share_near(u, p):
         below, above = index(column[u], y - 1, c), index(column[u], y + 1, c)
-        ring_arrived(u, side, 2, below, 1)
-        share_weight(u, side, 1, below)
-        ring_arrived(u, side, 3, above, 0)
-        share_weight(u, side, 2, above)
-
-    def share_far(u, side):
+        ring_arrived(u, p, 2, below, 1)
+        share_weight(u, p, 1, below)
+        ring_arrived(u, p, 3, above, 0)
+        share_weight(u, p, 2, above)
+
+    def share_far(u, p):
         far = index(column[u], y + 2, c)
-        ring_arrived(u, side, 4, far, 0)
-        ring_arrived(u, side, 5, far, 1)
-        share_weight(u, side, 3, far)
-
-    def from_sibling(u, side, k):
+        ring_arrived(u, p, 4, far, 0)
+        ring_arrived(u, p, 5, far, 1)
+        share_weight(u, p, 3, far)
+
+    def from_sibling(u, p, k):
         shift = (0, -1, 1, 2)[k]
-        arrived(weight_side(index(column[u], y + shift, 1 - c), side), pair_recv.at[u, side, k])
+        arrived(weight_piece(u, p, index(column[u], y + shift, 1 - c)), pair_recv.at[u, p, k])
 
     for j in range(EARLY):
         send_grad(j)
     loads[0].wait()
-    weight_rows(me)[...] = weights[...].astype(BF16)
-    for side in range(2):
-        ring_first(0, side, 0)
-        ring_first(0, side, 1)
-    for side in range(2):
-        share_weight(0, side, 0, me)
+    for p in range(2):
+        start, size = PIECES[0][p]
+        weight_piece(0, p, me)[...] = weights[:, start : start + size].astype(BF16)
+        ring_first(0, p, 0)
+        ring_first(0, p, 1)
+    for p in range(2):
+        share_weight(0, p, 0, me)
     for load in loads[6:]:
         load.start()
 
@@ -298,8 +314,7 @@
     send(other_rows, across_t, cross_send.at[0], cross_recv.at[0], device(across))
     for j in range(EARLY, CHUNKS):
         send_grad(j)
-    part = weight_side(me, 0)
-    send(part, part, cross_send.at[1], cross_recv.at[1], device(across))
+    cross_weight(0)
     lax.fori_loop(x * 2, x * 2 + 2, heads, 0)
     ring_second(0, 1)
 
@@ -412,19 +427,20 @@
             )
 
         def tile(n, carry):
-            at = pl.multiple_of(n * CHUNK, CHUNK)
+            at = pl.multiple_of(n * TILE, TILE)
             total = jnp.dot(
                 across_n[...],
-                every_weight[pl.ds(pl.multiple_of(x * 1024, 1024), 1024), pl.ds(SIDE + at, CHUNK)],
+                every_weight[pl.ds(pl.multiple_of(x * 1024, 1024), 1024), pl.ds(WHOLE + at, TILE)],
                 preferred_element_type=F32,
             )
-            out_sent[:, pl.ds(at, CHUNK)] = (total * SCALE).astype(BF16)
+            out_sent[:, pl.ds(at, TILE)] = (total * SCALE).astype(BF16)
             return carry
 
-        lax.fori_loop(0, SIDE // CHUNK, tile, 0)
+        lax.fori_loop(0, SHARED // TILE, tile, 0)
 
     def send_product(k):
-        at = pl.ds(k * CHUNK, CHUNK)
+        start, size = OUTS[1 + k]
+        at = pl.ds(start - WHOLE, size)
         send(out_sent.at[:, at], out_across.at[:, at], out_send.at[k], out_recv.at[k], device(across), late)
 
     for j in range(EARLY):
@@ -461,19 +477,16 @@
     update_chunk(CHUNKS - 2)
     share_group(2)
     update_chunk(CHUNKS - 1)
-    arrived(weight_side(across, 0), cross_recv.at[1])
-    ring_first(1, 0, 0)
-    ring_first(1, 0, 1)
-    share_weight(1, 0, 0, across)
+    take_weight(0)
     share_group(3)
-    for k in range(1, SIDE // CHUNK):
+    for k in range(1, 4):
         send_product(k)
     for group in range(3):
         outer_group(group)
 
     def multiply(tiles, spots, size, begin, finish):
         def tile(n, carry):
-            at = pl.ds(pl.multiple_of(n * CHUNK, CHUNK), CHUNK)
+            at = pl.ds(pl.multiple_of(n * TILE, TILE), TILE)
             total = None
             for spot in spots:
                 term = jnp.dot(
@@ -493,16 +506,19 @@
         lax.fori_loop(tiles[0], tiles[1], tile, 0)
 
     def store_out(k):
-        at = pl.ds(0, SIDE) if k == 0 else pl.ds(SIDE + (k - 1) * CHUNK, CHUNK)
-        return pltpu.make_async_copy(partial.at[0:SEQ, at], layer_out_hbm.at[:, at], store_sem.at[2 + k])
-
-    for k in range(4):
-        from_sibling(0, 0, k)
-    multiply((0, CHUNKS), [pl.multiple_of(x * 1024, 1024)], 1024, True, False)
-    outer_group(3)
-    ring_second(1, 0)
-    for item in started:
-        item.wait_send()
+        start, size = OUTS[k]
+        at = pl.ds(start, size)
+        store = pltpu.make_async_copy(partial.at[0:SEQ, at], layer_out_hbm.at[:, at], store_sem.at[k])
+        store.start()
+        stores.append(store)
+
+    def add_across(k):
+        start, size = OUTS[1 + k]
+        part, at = pl.ds(start - WHOLE, size), pl.ds(start, size)
+        arrived(out_across.at[:, part], out_recv.at[k])
+        for ref, spot in ((first, pl.ds(0, BLOCK)), (second, pl.ds(BLOCK, BLOCK))):
+            partial[spot, at] = (ref[:, at] * SCALE + out_across[spot, part].astype(F32)).astype(BF16)
+        store_out(1 + k)
 
     def outer_step(zz):
         spot = share_rows(zz)
@@ -511,37 +527,35 @@
         momentum[spot, :] = moved
         anchor[spot, :] = anchor[spot, :] - 0.7 * (delta + 0.9 * moved)
 
+    stores = []
+    for k in range(4):
+        from_sibling(0, 0, k)
+    multiply((0, D // TILE), [pl.multiple_of(x * 1024, 1024)], 1024, True, False)
+    outer_group(3)
+    ring_second(1, 0)
+    for item in started:
+        item.wait_send()
     outer_step(z)
     for zz in others:
         for group in range(CHUNKS // SENDS):
             arrived(outer.at[share_rows(zz), pl.ds(group * SPAN, SPAN)], outer_recv.at[zz, group])
         outer_step(zz)
-    stores = [
-        pltpu.make_async_copy(anchor, new_anchor_hbm, store_sem.at[0]),
-        pltpu.make_async_copy(momentum, new_momentum_hbm, store_sem.at[1]),
-    ]
-    for store in stores:
+    for n, ref in enumerate((anchor, momentum)):
+        store = pltpu.make_async_copy(ref, state_hbm.at[n * BLOCK : (n + 1) * BLOCK], store_sem.at[6 + n])
         store.start()
-
+        stores.append(store)
     share_near(1, 0)
     share_far(1, 0)
     for k in range(4):
         from_sibling(1, 0, k)
-    multiply((0, CHUNKS // 2), [pl.multiple_of((1 - x) * 1024, 1024)], 1024, False, True)
-    outs = [store_out(k) for k in range(5)]
-    outs[0].start()
-    for k in range(SIDE // CHUNK):
-        part, at = pl.ds(k * CHUNK, CHUNK), pl.ds(SIDE + k * CHUNK, CHUNK)
-        arrived(out_across.at[:, part], out_recv.at[k])
-        for ref, spot in ((first, pl.ds(0, BLOCK)), (second, pl.ds(BLOCK, BLOCK))):
-            partial[spot, at] = (ref[:, at] * SCALE + out_across[spot, part].astype(F32)).astype(BF16)
-        outs[k + 1].start()
+    multiply((0, WHOLE // TILE), [pl.multiple_of((1 - x) * 1024, 1024)], 1024, False, True)
+    store_out(0)
+    for k in range(4):
+        add_across(k)
     for item in late:
         item.wait_send()
     for store in stores:
         store.wait()
-    for out in outs:
-        out.wait()
 
 
 def on_device(
@@ -566,8 +580,8 @@
         pltpu.VMEM((WIDTH, SEQ), BF16),
         pltpu.VMEM((WIDTH // 2, SEQ), BF16),
         pltpu.VMEM((SEQ, WIDTH // 2), BF16),
-        pltpu.VMEM((SEQ, SIDE), BF16),
-        pltpu.VMEM((SEQ, SIDE), BF16),
+        pltpu.VMEM((SEQ, SHARED), BF16),
+        pltpu.VMEM((SEQ, SHARED), BF16),
         pltpu.VMEM((4 * HEAD, 4 * SEQ), BF16),
         pltpu.VMEM((4 * SEQ, D), BF16),
         pltpu.VMEM((WIDTH, D), BF16),
@@ -580,12 +594,12 @@
         pltpu.VMEM((4, SHARE, D), BF16),
         pltpu.VMEM((2, SHARE, D), BF16),
         pltpu.VMEM((BLOCK, D), BF16),
-        dma((11,)), dma((7,)),
+        dma((11,)), dma((8,)),
         dma((3, CHUNKS)), dma((3, CHUNKS)),
         dma((2, 4)), dma((2, 4)),
         dma((2, 2, 6)), dma((2, 2, 6)),
         dma((2, 2, 4)), dma((2, 2, 4)),
-        dma((2,)), dma((2,)),
+        dma((3,)), dma((3,)),
         dma((4,)), dma((4,)),
         dma((2, CHUNKS)), dma((2, CHUNKS)),
         dma((2, CHUNKS)), dma((2, CHUNKS)),
@@ -594,15 +608,14 @@
         dma((3, 4)), dma((4, 4)),
     ]
     anywhere = pl.BlockSpec(memory_space=pl.ANY)
-    return pl.pallas_call(
+    layer_out, state = pl.pallas_call(
         kernel,
         out_shape=(
             jax.ShapeDtypeStruct((SEQ, D), BF16),
-            jax.ShapeDtypeStruct((BLOCK, D), F32),
-            jax.ShapeDtypeStruct((BLOCK, D), F32),
+            jax.ShapeDtypeStruct((2 * BLOCK, D), F32),
         ),
         in_specs=[anywhere] * 11 + [pl.BlockSpec(memory_space=pltpu.SMEM)],
-        out_specs=(anywhere,) * 3,
+        out_specs=(anywhere,) * 2,
         scratch_shapes=scratch,
         compiler_params=pltpu.CompilerParams(
             collective_id=0, has_side_effects=True, vmem_limit_bytes=60 * 1024 * 1024
@@ -612,6 +625,7 @@
         queries, keys, values, log_decay, write_strength, out_grad, replica_weights,
         adam_first, adam_second, anchor, outer_momentum, exponents,
     )
+    return layer_out, state[:BLOCK], state[BLOCK:]
 
 
 def solution(mesh):

time: 118 us -> 117 us (level)
    unnamed x7 -> x3, local copies, waits for them, and re-layouts: 6.95 us -> 1.32 us
    slice x0 -> x1, local copies, waits for them, and re-layouts: none -> 4.83 us  [on_device(): return (layer_out, state[:BLOCK], state[BLOCK:])]
where the time goes in v3:
time: 117 us
  Pallas kernels  109 us (93%)
  local copies, waits for them, and re-layouts  6.16 us (5%)
  between operations  1.3 us (1%)
    pallas_call x1, Pallas kernels, on_device(): pl.pallas_call(kernel, out_shape=(jax.ShapeDtypeStruct((SEQ, D), BF16), j...  109 us
    slice x1, local copies, waits for them, and re-layouts, on_device(): return (layer_out, state[:BLOCK], state[BLOCK:])  4.83 us

profile of v3, /device:TPU:1, one launch (start us, length us, event | category | flops | bytes accessed | tf_op | source)
XLA Modules:
  0.0 116.6 jit_solution(2011170339296272042)
XLA Ops:
  1.3 109.2 %diloco_step.1 = (bf16[256,4096]{1,0:T(8,128)(2,1)}, f32[256,4096]{1,0:T(8,128)}) custom-call(bf16[256,2048]{1,0:T(8,128)(2,1)} %queries_hbm.1, bf16[256,2048]{1,0:T(8,128)(2,1)} %keys_hbm.1, bf16[256,2048]{1,0:T(8,128)(2,1)} %values_hbm.1, f32[16,256]{1,0:T(8,128)} %decay_hbm.1, f32[16,256]{1,0:T(8,128)} %strength_hbm.1, bf16[256,4096]{1,0:T(8,128)(2,1)} %out_grad_hbm.1, ...), custom_call_target="tpu_custom_call" | custom-call | tf_op jit(solution)/shard_map/diloco_step/pallas_call | solution.py:611
  110.5 0.0 copy-start
  110.5 4.8 %fusion = (f32[128,4096]{1,0:T(8,128)}, f32[128,4096]{1,0:T(8,128)}) fusion(f32[256,4096]{1,0:T(8,128)} %get-tuple-element.6), kind=kLoop, calls=%fused_computation | loop fusion | bytes 8388608 | tf_op jit(solution)/shard_map/slice | solution.py:628
  115.3 0.0 copy-done
  115.3 1.3 %copy.17 = bf16[256,4096]{1,0:T(8,128)(2,1)} copy(bf16[256,4096]{1,0:T(8,128)(2,1)S(1)} %copy-done) | data formatting | bytes 4194304
Async XLA Ops:
  110.5 4.8 %copy-start = (bf16[256,4096]{1,0:T(8,128)(2,1)S(1)}, bf16[256,4096]{1,0:T(8,128)(2,1)}, u32[]{:S(2)}) copy-start(bf16[256,4096]{1,0:T(8,128)(2,1)} %get-tuple-element.12) | copy-start | bytes 6291460

commit v4 on v3

--- a/solution.py
+++ b/solution.py
@@ -531,8 +531,8 @@
     for k in range(4):
         from_sibling(0, 0, k)
     multiply((0, D // TILE), [pl.multiple_of(x * 1024, 1024)], 1024, True, False)
+    ring_second(1, 0)
     outer_group(3)
-    ring_second(1, 0)
     for item in started:
         item.wait_send()
     outer_step(z)

time: 117 us -> 117 us (level)
  no operation moved by 1% of the time
where the time goes in v4:
time: 117 us
  Pallas kernels  109 us (93%)
  local copies, waits for them, and re-layouts  6.16 us (5%)
  between operations  1.3 us (1%)
    pallas_call x1, Pallas kernels, on_device(): pl.pallas_call(kernel, out_shape=(jax.ShapeDtypeStruct((SEQ, D), BF16), j...  109 us
    slice x1, local copies, waits for them, and re-layouts, on_device(): return (layer_out, state[:BLOCK], state[BLOCK:])  4.83 us

profile of v4, /device:TPU:1, one launch (start us, length us, event | category | flops | bytes accessed | tf_op | source)
XLA Modules:
  0.0 116.6 jit_solution(13034446211766250901)
XLA Ops:
  1.3 109.2 %diloco_step.1 = (bf16[256,4096]{1,0:T(8,128)(2,1)}, f32[256,4096]{1,0:T(8,128)}) custom-call(bf16[256,2048]{1,0:T(8,128)(2,1)} %queries_hbm.1, bf16[256,2048]{1,0:T(8,128)(2,1)} %keys_hbm.1, bf16[256,2048]{1,0:T(8,128)(2,1)} %values_hbm.1, f32[16,256]{1,0:T(8,128)} %decay_hbm.1, f32[16,256]{1,0:T(8,128)} %strength_hbm.1, bf16[256,4096]{1,0:T(8,128)(2,1)} %out_grad_hbm.1, ...), custom_call_target="tpu_custom_call" | custom-call | tf_op jit(solution)/shard_map/diloco_step/pallas_call | solution.py:611
  110.5 0.0 copy-start
  110.5 4.8 %fusion = (f32[128,4096]{1,0:T(8,128)}, f32[128,4096]{1,0:T(8,128)}) fusion(f32[256,4096]{1,0:T(8,128)} %get-tuple-element.6), kind=kLoop, calls=%fused_computation | loop fusion | bytes 8388608 | tf_op jit(solution)/shard_map/slice | solution.py:628
  115.3 0.0 copy-done
  115.3 1.3 %copy.17 = bf16[256,4096]{1,0:T(8,128)(2,1)} copy(bf16[256,4096]{1,0:T(8,128)(2,1)S(1)} %copy-done) | data formatting | bytes 4194304
Async XLA Ops:
  110.5 4.8 %copy-start = (bf16[256,4096]{1,0:T(8,128)(2,1)S(1)}, bf16[256,4096]{1,0:T(8,128)(2,1)}, u32[]{:S(2)}) copy-start(bf16[256,4096]{1,0:T(8,128)(2,1)} %get-tuple-element.12) | copy-start | bytes 6291460
